TPU v7x, 32 devices: a whole 2x2x4 slice. The times are simulated.
32 devices in a mesh: row: 8 (over z, x), col: 4 (over y, core).
Axes of the slice: x: 2, y: 2, z: 4, core: 2. Of those that a mesh axis runs over, the one named last changes fastest.
Arguments:
- marine_skin_quantities: float32 [5, 256, 512], P(None, 'row', 'col'), may hold values from -6 to 6
- marine_frozen_motion: float32 [2, 8, 16, 1024], P(None, 'row', 'col'), may hold values from -3 to 3
- floe_tensor_components: float32 [3, 8, 16, 1024], P(None, 'row', 'col'), may hold values from -3 to 3
- marine_frozen_weight: float32 [8, 16, 1024], P('row', 'col'), may hold values from 0.5 to 5
- floe_compressive_resistance: float32 [8, 16, 1024], P('row', 'col'), may hold values from 0.2 to 2
- ply_frozen_warmth: float32 [7, 8, 16, 1024], P(None, 'row', 'col'), may hold values from -15 to -2
- filled_places_each_chip: int32 [8, 4], P('row', 'col'), may hold values from 2 to 4, as said below
- frozen_presence_flags: int32 [8, 16], P('row', 'col'), may hold values from 0 to 1, as said below
- frozen_parent_grid_line: int32 [8, 16], P('row', 'col'), may hold values from -1 to 15, as said below
- adjacent_places: int32 [4, 8, 16], P(None, 'row', 'col'), may hold values from -1 to 127, as said below
Outputs:
- ice_velocity_new: float32 [2, 8, 16, 1024], P(None, 'row', 'col')
- ice_stress_new: float32 [3, 8, 16, 1024], P(None, 'row', 'col')
- ice_temperature_new: float32 [7, 8, 16, 1024], P(None, 'row', 'col')
- ocean_forcing: float32 [3, 256, 512], P(None, 'row', 'col')
Inputs may be any that keep to these rules, and one draw needn't show every extreme that they name: `filled_places_each_chip`: each device's count lies between 2 and 4; in every row some device has exactly 4. `frozen_presence_flags`: in each row of blocks the ice-covered blocks, in order of column, are dealt to the devices of that row in order, each device as many as its count. `frozen_parent_grid_line`: -1 marks slots beyond a device's count. A device's used slots hold, in order, consecutive ice-covered blocks of its row, all in its own ocean tile or in the tile just before it along col, at most 2 in the tile before; in every row some device holds exactly 2 from the tile before. `adjacent_places`: north is the next row of blocks, east the next block column (columns are periodic). -1 where the neighbor block is not ice-covered, lies beyond the first or last row of blocks, or the slot is unused.
All inputs are finite; a program needn't handle non-finite values.
Results may differ from a plain program's by a relative error of at most 0.0003.
Values sent between devices are 32-bit elements; how exact they have to be, the bound alone decides.
A program may use at most 64 MiB of HBM per device.

v0:
```python
import jax
import jax.numpy as jnp
from jax import lax
from jax.sharding import PartitionSpec as P

SUBCYCLES = 4


RELAX_RATE = 0.8
STEP_WEIGHT = 0.5
AIR_DRAG = 0.3
WATER_DRAG = 0.6
TOPMOST_WARMTH = -12.0
FREEZING = -1.8
DIFFUSION = 0.6
THERMAL_KAPPA = 0.1
OPEN_HEAT = 0.4
OPEN_WIND = 0.5


def from_behind(value, axis, steps):
    count = lax.axis_size(axis)
    leading, last = (max(0, -steps), min(count, count - steps))
    return lax.ppermute(value, axis, [(source, source + steps) for source in range(leading, last)])


def passed_along(x, axis, by):
    devices = lax.axis_size(axis)
    return lax.ppermute(x, axis, [(i, (i + by) % devices) for i in range(devices)])


def neighbor_values(field_values, halo_north, halo_south, halo_east, halo_west):
    boundary = halo_north.shape[-1]
    places = jnp.arange(field_values.shape[-1])
    grid_row = places // boundary
    grid_col = places % boundary
    repeats = (1,) * (field_values.ndim - 1) + (boundary,)
    upper_cells = jnp.where(
        grid_row == boundary - 1,
        jnp.tile(halo_north, repeats),
        jnp.roll(field_values, -boundary, axis=-1),
    )
    lower_cells = jnp.where(
        grid_row == 0, jnp.tile(halo_south, repeats), jnp.roll(field_values, boundary, axis=-1)
    )
    right_cells = jnp.where(
        grid_col == boundary - 1,
        jnp.repeat(halo_east, boundary, axis=-1),
        jnp.roll(field_values, -1, axis=-1),
    )
    left_cells = jnp.where(
        grid_col == 0, jnp.repeat(halo_west, boundary, axis=-1), jnp.roll(field_values, 1, axis=-1)
    )
    return (upper_cells, lower_cells, right_cells, left_cells)


def stress_update(floe_motion_speed, stress, strength, halo_set):
    upper_cells, lower_cells, right_cells, left_cells = neighbor_values(
        floe_motion_speed, halo_set[0], halo_set[1], halo_set[2], halo_set[3]
    )
    stretch_east = 0.5 * (right_cells[0] - left_cells[0])
    shear_east = 0.5 * (right_cells[1] - left_cells[1])
    shear_north = 0.5 * (upper_cells[0] - lower_cells[0])
    stretch_north = 0.5 * (upper_cells[1] - lower_cells[1])
    shearing = 0.5 * (shear_north + shear_east)
    divergence = stretch_east + stretch_north
    tension = stretch_east - stretch_north
    deformation = jnp.sqrt(
        divergence * divergence + 0.25 * (tension * tension + 4.0 * shearing * shearing) + 0.25
    )
    viscosity = strength / (2.0 * deformation)
    common = 0.75 * viscosity * divergence - 0.25 * strength
    target = jnp.stack(
        [
            0.5 * viscosity * stretch_east + common,
            0.5 * viscosity * stretch_north + common,
            0.5 * viscosity * shearing,
        ]
    )
    return (stress + RELAX_RATE * target) / (1.0 + RELAX_RATE)


def velocity_update(floe_motion_speed, stress, weight_density_sheet, skin_quantities, halo_set):
    upper_cells, lower_cells, right_cells, left_cells = neighbor_values(
        stress, halo_set[0], halo_set[1], halo_set[2], halo_set[3]
    )
    force_east = 0.5 * (right_cells[0] - left_cells[0]) + 0.5 * (upper_cells[2] - lower_cells[2])
    force_north = 0.5 * (right_cells[2] - left_cells[2]) + 0.5 * (upper_cells[1] - lower_cells[1])
    pushing = (
        jnp.stack([force_east, force_north])
        + AIR_DRAG * skin_quantities[3:5]
        + WATER_DRAG * skin_quantities[1:3]
    )
    return (weight_density_sheet * floe_motion_speed + STEP_WEIGHT * pushing) / (
        weight_density_sheet + STEP_WEIGHT * WATER_DRAG
    )


def thermal_diffusive_update(ply_warmth_state, weight_density_sheet, skin_quantities):
    floe_depth_extent = weight_density_sheet / 0.9
    marine_exchange_step = DIFFUSION / (floe_depth_extent * floe_depth_extent)
    diagonal = 1.0 + 2.0 * marine_exchange_step
    ply_sequence = ply_warmth_state.shape[0]
    ratios = []
    partial_values = []
    for depthwise_ply_number in range(ply_sequence):
        warming_supply_rate = ply_warmth_state[depthwise_ply_number]
        if depthwise_ply_number == 0:
            warming_supply_rate = warming_supply_rate + marine_exchange_step * TOPMOST_WARMTH
        if depthwise_ply_number == ply_sequence - 1:
            warming_supply_rate = warming_supply_rate + marine_exchange_step * skin_quantities[0]
        if depthwise_ply_number == 0:
            pivot_value = diagonal
            carried = warming_supply_rate / pivot_value
        else:
            pivot_value = diagonal - marine_exchange_step * ratios[-1]
            carried = (
                warming_supply_rate + marine_exchange_step * partial_values[-1]
            ) / pivot_value
        ratios.append(marine_exchange_step / pivot_value)
        partial_values.append(carried)
    solved = [partial_values[-1]]
    for depthwise_ply_number in range(ply_sequence - 2, -1, -1):
        solved.insert(
            0, partial_values[depthwise_ply_number] + ratios[depthwise_ply_number] * solved[0]
        )
    return jnp.stack(solved)


def marine_frozen_exchanges(
    ply_warmth_state, floe_motion_speed, weight_density_sheet, skin_quantities
):
    floe_depth_extent = weight_density_sheet / 0.9
    thermal_transfer_amount = (
        THERMAL_KAPPA * (ply_warmth_state[-1] - skin_quantities[0]) / floe_depth_extent
    )
    return jnp.concatenate(
        [thermal_transfer_amount[None], WATER_DRAG * (floe_motion_speed - skin_quantities[1:3])],
        axis=0,
    )


def open_water(skin_quantities):
    thermal_transfer_amount = -OPEN_HEAT * (skin_quantities[0] - FREEZING)
    return jnp.concatenate(
        [thermal_transfer_amount[None], OPEN_WIND * skin_quantities[3:5]], axis=0
    )


def to_blocks(ocean_tile, boundary):
    fields = ocean_tile.shape[0]
    per_tile = ocean_tile.shape[2] // boundary
    return (
        ocean_tile.reshape(fields, boundary, per_tile, boundary)
        .transpose(0, 2, 1, 3)
        .reshape(fields, per_tile, boundary * boundary)
    )


def gather_from_blocks(block_values, boundary):
    fields = block_values.shape[0]
    block_total = block_values.shape[1]
    return (
        block_values.reshape(fields, block_total, boundary, boundary)
        .transpose(0, 2, 1, 3)
        .reshape(fields, boundary, block_total * boundary)
    )


def local(
    marine_skin_quantities,
    marine_frozen_motion,
    floe_tensor_components,
    marine_frozen_weight,
    floe_compressive_resistance,
    ply_frozen_warmth,
    filled_places_each_chip,
    frozen_presence_flags,
    frozen_parent_grid_line,
    adjacent_places,
):
    boundary = marine_skin_quantities.shape[1]
    tile_blocks = marine_skin_quantities.shape[2] // boundary
    slots_here = marine_frozen_motion.shape[2]
    cell_count = marine_frozen_motion.shape[3]
    col_index = lax.axis_index("col")
    col_count = lax.axis_size("col")
    first_block = tile_blocks * col_index
    floe_motion_speed = marine_frozen_motion[:, 0]
    stress = floe_tensor_components[:, 0]
    weight_density_sheet = marine_frozen_weight[0]
    strength = floe_compressive_resistance[0]
    ply_warmth_state = ply_frozen_warmth[:, 0]
    source = frozen_parent_grid_line[0]
    slot_range = jnp.arange(slots_here, dtype=jnp.int32)
    slot_alive = slot_range < filled_places_each_chip[0, 0]
    covered = frozen_presence_flags[0]
    own_blocks = to_blocks(marine_skin_quantities, boundary)
    earlier = from_behind(marine_skin_quantities, "col", 1)
    candidates = jnp.concatenate([to_blocks(earlier, boundary), own_blocks], axis=1)
    chosen_index = jnp.clip(source - first_block + tile_blocks, 0, 2 * tile_blocks - 1)
    skin_quantities = jnp.take(candidates, chosen_index, axis=1)
    link_ids = adjacent_places[:, 0, :]
    slots_row = slots_here * col_count
    remainder = link_ids % slots_row
    link_col = remainder // slots_here
    link_slot = remainder % slots_here
    offset = (link_col - col_index + 2) % col_count - 2
    planes = jnp.array([3, 2, 1, 0], dtype=jnp.int32)[:, None]
    window_index = jnp.clip(
        ((offset + 2) * 4 + planes) * slots_here + link_slot, 0, 20 * slots_here - 1
    )
    linked = link_ids >= 0

    def edge_halos(field_values):
        fields = field_values.shape[0]
        square = field_values.reshape(fields, slots_here, boundary, boundary)
        received = []
        for shift_by, edge_strip in ((1, square[:, :, boundary - 1, :]), (-1, square[:, :, 0, :])):
            received.append(from_behind(edge_strip, "row", shift_by))
        stacked = jnp.stack(
            [square[:, :, :, boundary - 1], square[:, :, :, 0], received[0], received[1]]
        )
        window = [
            stacked if col_reach == 0 else passed_along(stacked, "col", -col_reach)
            for col_reach in (-2, -1, 0, 1, 2)
        ]
        assembled = (
            jnp.stack(window).transpose(2, 0, 1, 3, 4).reshape(fields, 20 * slots_here, boundary)
        )
        fetched = jnp.take(assembled, window_index, axis=1)
        fetched = jnp.where(linked[None, :, :, None], fetched, 0.0)
        return (fetched[:, 0], fetched[:, 1], fetched[:, 2], fetched[:, 3])

    for step_index in range(SUBCYCLES):
        stress = stress_update(floe_motion_speed, stress, strength, edge_halos(floe_motion_speed))
        floe_motion_speed = velocity_update(
            floe_motion_speed, stress, weight_density_sheet, skin_quantities, edge_halos(stress)
        )
    ply_warmth_state = thermal_diffusive_update(
        ply_warmth_state, weight_density_sheet, skin_quantities
    )
    skin_exchanges = marine_frozen_exchanges(
        ply_warmth_state, floe_motion_speed, weight_density_sheet, skin_quantities
    )
    target_spot = jnp.where(slot_alive, source - first_block + tile_blocks, 2 * tile_blocks)
    gathered = (
        jnp.zeros((3, 2 * tile_blocks, cell_count), jnp.float32)
        .at[:, target_spot]
        .add(skin_exchanges, mode="drop")
    )
    returned = from_behind(gathered[:, :tile_blocks], "col", -1)
    ice_flux = gathered[:, tile_blocks:] + returned
    applied_driving_load = jnp.where(
        (covered == 1)[None, :, None], ice_flux, open_water(own_blocks)
    )
    keep_flags = slot_alive[None, :, None]
    motion_result = jnp.where(keep_flags, floe_motion_speed, 0.0)[:, None]
    tensor_result = jnp.where(keep_flags, stress, 0.0)[:, None]
    warmth_result = jnp.where(keep_flags, ply_warmth_state, 0.0)[:, None]
    return (
        motion_result,
        tensor_result,
        warmth_result,
        gather_from_blocks(applied_driving_load, boundary),
    )


def solution(mesh):
    in_specs = (
        P(None, "row", "col"),
        P(None, "row", "col", None),
        P(None, "row", "col", None),
        P("row", "col", None),
        P("row", "col", None),
        P(None, "row", "col", None),
        P("row", "col"),
        P("row", "col"),
        P("row", "col"),
        P(None, "row", "col"),
    )
    out_specs = (
        P(None, "row", "col", None),
        P(None, "row", "col", None),
        P(None, "row", "col", None),
        P(None, "row", "col"),
    )
    return jax.shard_map(local, mesh=mesh, in_specs=in_specs, out_specs=out_specs, check_vma=False)
```

profile of v0, /device:TPU:25, one launch (start us, length us, event | category | flops | bytes accessed | tf_op | source)
XLA Modules:
  0.0 147.6 jit_solution(15376583830879711738)
XLA Ops:
  0.6 3.8 %collective-permute-start.10 = (f32[5,32,128]{2,1,0:T(8,128)}, f32[5,32,128]{2,1,0:T(8,128)S(1)}, u32[]{:S(2)}, u32[]{:S(2)}) collective-permute-start(f32[5,32,128]{2,1,0:T(8,128)} %param.15), channel_id=1, source_target_pairs={{0,1},{1,2},{2,3},{4,5},{5,6},{6,7},{8,9},{9,10},{10,11},{12,13},{... | collective-permute-start | bytes 245768 | tf_op jit(solution)/shard_map/ppermute | solution.py:24
  5.4 3.0 %collective-permute-start.1 = (f32[2,4,32]{2,1,0:T(4,128)S(1)}, f32[2,4,32]{2,1,0:T(4,128)S(1)}, u32[]{:S(2)}, u32[]{:S(2)}) collective-permute-start(f32[2,4,32]{2,1,0:T(4,128)S(1)} %bitcast.671), channel_id=1, source_target_pairs={{4,0},{8,4},{12,8},{16,12},{20,16},{24,20},{28,24},{5,1},{9,5},{13... | collective-permute-start | bytes 3080 | tf_op jit(solution)/shard_map/ppermute | solution.py:24
  8.4 2.3 %collective-permute-start = (f32[2,4,32]{2,1,0:T(4,128)S(1)}, f32[2,4,32]{2,1,0:T(4,128)S(1)}, u32[]{:S(2)}, u32[]{:S(2)}) collective-permute-start(f32[2,4,32]{2,1,0:T(4,128)S(1)} %bitcast.670), channel_id=1, source_target_pairs={{0,4},{4,8},{8,12},{12,16},{16,20},{20,24},{24,28},{1,5},{5,9},{9,... | collective-permute-start | bytes 3080 | tf_op jit(solution)/shard_map/ppermute | solution.py:24
  17.8 2.3 %collective-permute-done.4 = f32[4,2,4,32]{3,2,0,1:T(4,128)S(1)} collective-permute-done((f32[4,2,4,32]{3,2,0,1:T(4,128)S(1)}, f32[4,2,4,32]{3,2,0,1:T(4,128)S(1)}, u32[]{:S(2)}, u32[]{:S(2)}) %collective-permute-start.4) | collective-permute-done | bytes 4128 | tf_op jit(solution)/shard_map/ppermute | solution.py:29
  23.7 3.5 %collective-permute-start.6 = (f32[3,4,32]{2,1,0:T(4,128)S(1)}, f32[3,4,32]{2,1,0:T(4,128)S(1)}, u32[]{:S(2)}, u32[]{:S(2)}) collective-permute-start(f32[3,4,32]{2,1,0:T(4,128)S(1)} %bitcast.659), channel_id=1, source_target_pairs={{4,0},{8,4},{12,8},{16,12},{20,16},{24,20},{28,24},{5,1},{9,5},{13... | collective-permute-start | bytes 4616 | tf_op jit(solution)/shard_map/ppermute | solution.py:24
  27.2 1.9 %collective-permute-start.5 = (f32[3,4,32]{2,1,0:T(4,128)S(1)}, f32[3,4,32]{2,1,0:T(4,128)S(1)}, u32[]{:S(2)}, u32[]{:S(2)}) collective-permute-start(f32[3,4,32]{2,1,0:T(4,128)S(1)} %bitcast.656), channel_id=1, source_target_pairs={{0,4},{4,8},{8,12},{12,16},{16,20},{20,24},{24,28},{1,5},{5,9},{9,... | collective-permute-start | bytes 4616 | tf_op jit(solution)/shard_map/ppermute | solution.py:24
  29.5 3.0 %collective-permute-done.5 = f32[3,4,32]{2,1,0:T(4,128)S(1)} collective-permute-done((f32[3,4,32]{2,1,0:T(4,128)S(1)}, f32[3,4,32]{2,1,0:T(4,128)S(1)}, u32[]{:S(2)}, u32[]{:S(2)}) %collective-permute-start.5) | collective-permute-done | bytes 1568 | tf_op jit(solution)/shard_map/ppermute | solution.py:24
  34.0 1.8 %collective-permute-start.8 = (f32[4,3,4,32]{3,2,1,0:T(4,128)S(1)}, f32[4,3,4,32]{3,2,1,0:T(4,128)S(1)}, u32[]{:S(2)}, u32[]{:S(2)}) collective-permute-start(f32[4,3,4,32]{3,2,1,0:T(4,128)S(1)} %pad_maximum_fusion.1), channel_id=1, source_target_pairs={{0,1},{1,2},{2,3},{3,0},{4,5},{5,6},{6,7},{7,4},{8,9},{9,10},{10,1... | collective-permute-start | bytes 18440 | tf_op jit(solution)/shard_map/ppermute | solution.py:29
  36.8 2.3 %collective-permute-done.9 = f32[4,3,4,32]{3,2,1,0:T(4,128)S(1)} collective-permute-done((f32[4,3,4,32]{3,2,1,0:T(4,128)S(1)}, f32[4,3,4,32]{3,2,1,0:T(4,128)S(1)}, u32[]{:S(2)}, u32[]{:S(2)}) %collective-permute-start.9) | collective-permute-done | bytes 6176 | tf_op jit(solution)/shard_map/ppermute | solution.py:29
  42.9 1.9 %collective-permute-start.12 = (f32[2,4,32]{2,1,0:T(4,128)S(1)}, f32[2,4,32]{2,1,0:T(4,128)S(1)}, u32[]{:S(2)}, u32[]{:S(2)}) collective-permute-start(f32[2,4,32]{2,1,0:T(4,128)S(1)} %bitcast.664), channel_id=1, source_target_pairs={{4,0},{8,4},{12,8},{16,12},{20,16},{24,20},{28,24},{5,1},{9,5},{13... | collective-permute-start | bytes 3080 | tf_op jit(solution)/shard_map/ppermute | solution.py:24
  44.9 3.4 %collective-permute-start.11 = (f32[2,4,32]{2,1,0:T(4,128)S(1)}, f32[2,4,32]{2,1,0:T(4,128)S(1)}, u32[]{:S(2)}, u32[]{:S(2)}) collective-permute-start(f32[2,4,32]{2,1,0:T(4,128)S(1)} %bitcast.665), channel_id=1, source_target_pairs={{0,4},{4,8},{8,12},{12,16},{16,20},{20,24},{24,28},{1,5},{5,9},{9,... | collective-permute-start | bytes 3080 | tf_op jit(solution)/shard_map/ppermute | solution.py:24
  51.1 1.8 %collective-permute-start.14 = (f32[4,2,4,32]{3,2,0,1:T(4,128)S(1)}, f32[4,2,4,32]{3,2,0,1:T(4,128)S(1)}, u32[]{:S(2)}, u32[]{:S(2)}) collective-permute-start(f32[4,2,4,32]{3,2,0,1:T(4,128)S(1)} %pad_maximum_fusion.6), channel_id=1, source_target_pairs={{0,1},{1,2},{2,3},{3,0},{4,5},{5,6},{6,7},{7,4},{8,9},{9,10},{10,1... | collective-permute-start | bytes 12296 | tf_op jit(solution)/shard_map/ppermute | solution.py:29
  53.7 2.3 %collective-permute-done.15 = f32[4,2,4,32]{3,2,0,1:T(4,128)S(1)} collective-permute-done((f32[4,2,4,32]{3,2,0,1:T(4,128)S(1)}, f32[4,2,4,32]{3,2,0,1:T(4,128)S(1)}, u32[]{:S(2)}, u32[]{:S(2)}) %collective-permute-start.15) | collective-permute-done | bytes 4128 | tf_op jit(solution)/shard_map/ppermute | solution.py:29
  59.1 2.6 %collective-permute-start.17 = (f32[3,4,32]{2,1,0:T(4,128)S(1)}, f32[3,4,32]{2,1,0:T(4,128)S(1)}, u32[]{:S(2)}, u32[]{:S(2)}) collective-permute-start(f32[3,4,32]{2,1,0:T(4,128)S(1)} %bitcast.660), channel_id=1, source_target_pairs={{4,0},{8,4},{12,8},{16,12},{20,16},{24,20},{28,24},{5,1},{9,5},{13... | collective-permute-start | bytes 4616 | tf_op jit(solution)/shard_map/ppermute | solution.py:24
  61.7 2.6 %collective-permute-start.16 = (f32[3,4,32]{2,1,0:T(4,128)S(1)}, f32[3,4,32]{2,1,0:T(4,128)S(1)}, u32[]{:S(2)}, u32[]{:S(2)}) collective-permute-start(f32[3,4,32]{2,1,0:T(4,128)S(1)} %bitcast.657), channel_id=1, source_target_pairs={{0,4},{4,8},{8,12},{12,16},{16,20},{20,24},{24,28},{1,5},{5,9},{9,... | collective-permute-start | bytes 4616 | tf_op jit(solution)/shard_map/ppermute | solution.py:24
  64.7 2.3 %collective-permute-done.16 = f32[3,4,32]{2,1,0:T(4,128)S(1)} collective-permute-done((f32[3,4,32]{2,1,0:T(4,128)S(1)}, f32[3,4,32]{2,1,0:T(4,128)S(1)}, u32[]{:S(2)}, u32[]{:S(2)}) %collective-permute-start.16) | collective-permute-done | bytes 1568 | tf_op jit(solution)/shard_map/ppermute | solution.py:24
  71.0 2.3 %collective-permute-done.20 = f32[4,3,4,32]{3,2,1,0:T(4,128)S(1)} collective-permute-done((f32[4,3,4,32]{3,2,1,0:T(4,128)S(1)}, f32[4,3,4,32]{3,2,1,0:T(4,128)S(1)}, u32[]{:S(2)}, u32[]{:S(2)}) %collective-permute-start.20) | collective-permute-done | bytes 6176 | tf_op jit(solution)/shard_map/ppermute | solution.py:29
  76.0 1.9 %collective-permute-start.22 = (f32[2,4,32]{2,1,0:T(4,128)S(1)}, f32[2,4,32]{2,1,0:T(4,128)S(1)}, u32[]{:S(2)}, u32[]{:S(2)}) collective-permute-start(f32[2,4,32]{2,1,0:T(4,128)S(1)} %bitcast.666), channel_id=1, source_target_pairs={{4,0},{8,4},{12,8},{16,12},{20,16},{24,20},{28,24},{5,1},{9,5},{13... | collective-permute-start | bytes 3080 | tf_op jit(solution)/shard_map/ppermute | solution.py:24
  78.0 3.4 %collective-permute-start.21 = (f32[2,4,32]{2,1,0:T(4,128)S(1)}, f32[2,4,32]{2,1,0:T(4,128)S(1)}, u32[]{:S(2)}, u32[]{:S(2)}) collective-permute-start(f32[2,4,32]{2,1,0:T(4,128)S(1)} %bitcast.668), channel_id=1, source_target_pairs={{0,4},{4,8},{8,12},{12,16},{16,20},{20,24},{24,28},{1,5},{5,9},{9,... | collective-permute-start | bytes 3080 | tf_op jit(solution)/shard_map/ppermute | solution.py:24
  86.2 2.3 %collective-permute-done.25 = f32[4,2,4,32]{3,2,0,1:T(4,128)S(1)} collective-permute-done((f32[4,2,4,32]{3,2,0,1:T(4,128)S(1)}, f32[4,2,4,32]{3,2,0,1:T(4,128)S(1)}, u32[]{:S(2)}, u32[]{:S(2)}) %collective-permute-start.25) | collective-permute-done | bytes 4128 | tf_op jit(solution)/shard_map/ppermute | solution.py:29
  91.7 2.6 %collective-permute-start.27 = (f32[3,4,32]{2,1,0:T(4,128)S(1)}, f32[3,4,32]{2,1,0:T(4,128)S(1)}, u32[]{:S(2)}, u32[]{:S(2)}) collective-permute-start(f32[3,4,32]{2,1,0:T(4,128)S(1)} %bitcast.661), channel_id=1, source_target_pairs={{4,0},{8,4},{12,8},{16,12},{20,16},{24,20},{28,24},{5,1},{9,5},{13... | collective-permute-start | bytes 4616 | tf_op jit(solution)/shard_map/ppermute | solution.py:24
  94.3 2.7 %collective-permute-start.26 = (f32[3,4,32]{2,1,0:T(4,128)S(1)}, f32[3,4,32]{2,1,0:T(4,128)S(1)}, u32[]{:S(2)}, u32[]{:S(2)}) collective-permute-start(f32[3,4,32]{2,1,0:T(4,128)S(1)} %bitcast.658), channel_id=1, source_target_pairs={{0,4},{4,8},{8,12},{12,16},{16,20},{20,24},{24,28},{1,5},{5,9},{9,... | collective-permute-start | bytes 4616 | tf_op jit(solution)/shard_map/ppermute | solution.py:24
  97.3 2.2 %collective-permute-done.26 = f32[3,4,32]{2,1,0:T(4,128)S(1)} collective-permute-done((f32[3,4,32]{2,1,0:T(4,128)S(1)}, f32[3,4,32]{2,1,0:T(4,128)S(1)}, u32[]{:S(2)}, u32[]{:S(2)}) %collective-permute-start.26) | collective-permute-done | bytes 1568 | tf_op jit(solution)/shard_map/ppermute | solution.py:24
  103.5 2.3 %collective-permute-done.30 = f32[4,3,4,32]{3,2,1,0:T(4,128)S(1)} collective-permute-done((f32[4,3,4,32]{3,2,1,0:T(4,128)S(1)}, f32[4,3,4,32]{3,2,1,0:T(4,128)S(1)}, u32[]{:S(2)}, u32[]{:S(2)}) %collective-permute-start.30) | collective-permute-done | bytes 6176 | tf_op jit(solution)/shard_map/ppermute | solution.py:29
  108.5 1.9 %collective-permute-start.32 = (f32[2,4,32]{2,1,0:T(4,128)S(1)}, f32[2,4,32]{2,1,0:T(4,128)S(1)}, u32[]{:S(2)}, u32[]{:S(2)}) collective-permute-start(f32[2,4,32]{2,1,0:T(4,128)S(1)} %bitcast.667), channel_id=1, source_target_pairs={{4,0},{8,4},{12,8},{16,12},{20,16},{24,20},{28,24},{5,1},{9,5},{13... | collective-permute-start | bytes 3080 | tf_op jit(solution)/shard_map/ppermute | solution.py:24
  110.4 3.4 %collective-permute-start.31 = (f32[2,4,32]{2,1,0:T(4,128)S(1)}, f32[2,4,32]{2,1,0:T(4,128)S(1)}, u32[]{:S(2)}, u32[]{:S(2)}) collective-permute-start(f32[2,4,32]{2,1,0:T(4,128)S(1)} %bitcast.669), channel_id=1, source_target_pairs={{0,4},{4,8},{8,12},{12,16},{16,20},{20,24},{24,28},{1,5},{5,9},{9,... | collective-permute-start | bytes 3080 | tf_op jit(solution)/shard_map/ppermute | solution.py:24
  118.6 2.3 %collective-permute-done.35 = f32[4,2,4,32]{3,2,0,1:T(4,128)S(1)} collective-permute-done((f32[4,2,4,32]{3,2,0,1:T(4,128)S(1)}, f32[4,2,4,32]{3,2,0,1:T(4,128)S(1)}, u32[]{:S(2)}, u32[]{:S(2)}) %collective-permute-start.35) | collective-permute-done | bytes 4128 | tf_op jit(solution)/shard_map/ppermute | solution.py:29
  124.1 1.9 %collective-permute-start.37 = (f32[3,4,32]{2,1,0:T(4,128)S(1)}, f32[3,4,32]{2,1,0:T(4,128)S(1)}, u32[]{:S(2)}, u32[]{:S(2)}) collective-permute-start(f32[3,4,32]{2,1,0:T(4,128)S(1)} %bitcast.663), channel_id=1, source_target_pairs={{4,0},{8,4},{12,8},{16,12},{20,16},{24,20},{28,24},{5,1},{9,5},{13... | collective-permute-start | bytes 4616 | tf_op jit(solution)/shard_map/ppermute | solution.py:24
  126.1 3.4 %collective-permute-start.36 = (f32[3,4,32]{2,1,0:T(4,128)S(1)}, f32[3,4,32]{2,1,0:T(4,128)S(1)}, u32[]{:S(2)}, u32[]{:S(2)}) collective-permute-start(f32[3,4,32]{2,1,0:T(4,128)S(1)} %bitcast.662), channel_id=1, source_target_pairs={{0,4},{4,8},{8,12},{12,16},{16,20},{20,24},{24,28},{1,5},{5,9},{9,... | collective-permute-start | bytes 4616 | tf_op jit(solution)/shard_map/ppermute | solution.py:24
  135.6 2.3 %collective-permute-done.40 = f32[4,3,4,32]{3,2,1,0:T(4,128)S(1)} collective-permute-done((f32[4,3,4,32]{3,2,1,0:T(4,128)S(1)}, f32[4,3,4,32]{3,2,1,0:T(4,128)S(1)}, u32[]{:S(2)}, u32[]{:S(2)}) %collective-permute-start.40) | collective-permute-done | bytes 6176 | tf_op jit(solution)/shard_map/ppermute | solution.py:29
  140.9 1.9 %collective-permute-start.41 = (f32[3,4,1024]{2,0,1:T(4,128)S(1)}, f32[3,4,1024]{2,0,1:T(4,128)S(1)}, u32[]{:S(2)}, u32[]{:S(2)}) collective-permute-start(f32[3,4,1024]{2,0,1:T(4,128)S(1)} %slice.1071), channel_id=1, source_target_pairs={{1,0},{2,1},{3,2},{5,4},{6,5},{7,6},{9,8},{10,9},{11,10},{13,12},{... | collective-permute-start | bytes 147464 | tf_op jit(solution)/shard_map/ppermute | solution.py:24
  143.6 2.9 %collective-permute-done.41 = f32[3,4,1024]{2,0,1:T(4,128)S(1)} collective-permute-done((f32[3,4,1024]{2,0,1:T(4,128)S(1)}, f32[3,4,1024]{2,0,1:T(4,128)S(1)}, u32[]{:S(2)}, u32[]{:S(2)}) %collective-permute-start.41) | collective-permute-done | bytes 49184 | tf_op jit(solution)/shard_map/ppermute | solution.py:24
  (451 shorter events, 64.1 us)
Async XLA Ops:
  0.6 40.6 %collective-permute-start.10 = (f32[5,32,128]{2,1,0:T(8,128)}, f32[5,32,128]{2,1,0:T(8,128)S(1)}, u32[]{:S(2)}, u32[]{:S(2)}) collective-permute-start(f32[5,32,128]{2,1,0:T(8,128)} %param.15), channel_id=1, source_target_pairs={{0,1},{1,2},{2,3},{4,5},{5,6},{6,7},{8,9},{9,10},{10,11},{12,13},{... | collective-permute-start | bytes 245768 | tf_op jit(solution)/shard_map/ppermute | solution.py:24
  5.4 8.7 %collective-permute-start.1 = (f32[2,4,32]{2,1,0:T(4,128)S(1)}, f32[2,4,32]{2,1,0:T(4,128)S(1)}, u32[]{:S(2)}, u32[]{:S(2)}) collective-permute-start(f32[2,4,32]{2,1,0:T(4,128)S(1)} %bitcast.671), channel_id=1, source_target_pairs={{4,0},{8,4},{12,8},{16,12},{20,16},{24,20},{28,24},{5,1},{9,5},{13... | collective-permute-start | bytes 3080 | tf_op jit(solution)/shard_map/ppermute | solution.py:24
  8.4 5.7 %collective-permute-start = (f32[2,4,32]{2,1,0:T(4,128)S(1)}, f32[2,4,32]{2,1,0:T(4,128)S(1)}, u32[]{:S(2)}, u32[]{:S(2)}) collective-permute-start(f32[2,4,32]{2,1,0:T(4,128)S(1)} %bitcast.670), channel_id=1, source_target_pairs={{0,4},{4,8},{8,12},{12,16},{16,20},{20,24},{24,28},{1,5},{5,9},{9,... | collective-permute-start | bytes 3080 | tf_op jit(solution)/shard_map/ppermute | solution.py:24
  14.1 3.0 %collective-permute-start.2 = (f32[4,2,4,32]{3,2,0,1:T(4,128)S(1)}, f32[4,2,4,32]{3,2,0,1:T(4,128)S(1)}, u32[]{:S(2)}, u32[]{:S(2)}) collective-permute-start(f32[4,2,4,32]{3,2,0,1:T(4,128)S(1)} %pad_maximum_fusion.5), channel_id=1, source_target_pairs={{0,2},{1,3},{2,0},{3,1},{4,6},{5,7},{6,4},{7,5},{8,10},{9,11},{10,... | collective-permute-start | bytes 12296 | tf_op jit(solution)/shard_map/ppermute | solution.py:29
  16.9 3.2 %collective-permute-start.4 = (f32[4,2,4,32]{3,2,0,1:T(4,128)S(1)}, f32[4,2,4,32]{3,2,0,1:T(4,128)S(1)}, u32[]{:S(2)}, u32[]{:S(2)}) collective-permute-start(f32[4,2,4,32]{3,2,0,1:T(4,128)S(1)} %pad_maximum_fusion.5), channel_id=1, source_target_pairs={{0,3},{1,0},{2,1},{3,2},{4,7},{5,4},{6,5},{7,6},{8,11},{9,8},{10,9... | collective-permute-start | bytes 12296 | tf_op jit(solution)/shard_map/ppermute | solution.py:29
  23.7 5.8 %collective-permute-start.6 = (f32[3,4,32]{2,1,0:T(4,128)S(1)}, f32[3,4,32]{2,1,0:T(4,128)S(1)}, u32[]{:S(2)}, u32[]{:S(2)}) collective-permute-start(f32[3,4,32]{2,1,0:T(4,128)S(1)} %bitcast.659), channel_id=1, source_target_pairs={{4,0},{8,4},{12,8},{16,12},{20,16},{24,20},{28,24},{5,1},{9,5},{13... | collective-permute-start | bytes 4616 | tf_op jit(solution)/shard_map/ppermute | solution.py:24
  27.2 5.3 %collective-permute-start.5 = (f32[3,4,32]{2,1,0:T(4,128)S(1)}, f32[3,4,32]{2,1,0:T(4,128)S(1)}, u32[]{:S(2)}, u32[]{:S(2)}) collective-permute-start(f32[3,4,32]{2,1,0:T(4,128)S(1)} %bitcast.656), channel_id=1, source_target_pairs={{0,4},{4,8},{8,12},{12,16},{16,20},{20,24},{24,28},{1,5},{5,9},{9,... | collective-permute-start | bytes 4616 | tf_op jit(solution)/shard_map/ppermute | solution.py:24
  32.5 3.3 %collective-permute-start.7 = (f32[4,3,4,32]{3,2,1,0:T(4,128)S(1)}, f32[4,3,4,32]{3,2,1,0:T(4,128)S(1)}, u32[]{:S(2)}, u32[]{:S(2)}) collective-permute-start(f32[4,3,4,32]{3,2,1,0:T(4,128)S(1)} %pad_maximum_fusion.1), channel_id=1, source_target_pairs={{0,2},{1,3},{2,0},{3,1},{4,6},{5,7},{6,4},{7,5},{8,10},{9,11},{10,... | collective-permute-start | bytes 18440 | tf_op jit(solution)/shard_map/ppermute | solution.py:29
  34.0 2.7 %collective-permute-start.8 = (f32[4,3,4,32]{3,2,1,0:T(4,128)S(1)}, f32[4,3,4,32]{3,2,1,0:T(4,128)S(1)}, u32[]{:S(2)}, u32[]{:S(2)}) collective-permute-start(f32[4,3,4,32]{3,2,1,0:T(4,128)S(1)} %pad_maximum_fusion.1), channel_id=1, source_target_pairs={{0,1},{1,2},{2,3},{3,0},{4,5},{5,6},{6,7},{7,4},{8,9},{9,10},{10,1... | collective-permute-start | bytes 18440 | tf_op jit(solution)/shard_map/ppermute | solution.py:29
  35.8 3.3 %collective-permute-start.9 = (f32[4,3,4,32]{3,2,1,0:T(4,128)S(1)}, f32[4,3,4,32]{3,2,1,0:T(4,128)S(1)}, u32[]{:S(2)}, u32[]{:S(2)}) collective-permute-start(f32[4,3,4,32]{3,2,1,0:T(4,128)S(1)} %pad_maximum_fusion.1), channel_id=1, source_target_pairs={{0,3},{1,0},{2,1},{3,2},{4,7},{5,4},{6,5},{7,6},{8,11},{9,8},{10,9... | collective-permute-start | bytes 18440 | tf_op jit(solution)/shard_map/ppermute | solution.py:29
  42.9 6.5 %collective-permute-start.12 = (f32[2,4,32]{2,1,0:T(4,128)S(1)}, f32[2,4,32]{2,1,0:T(4,128)S(1)}, u32[]{:S(2)}, u32[]{:S(2)}) collective-permute-start(f32[2,4,32]{2,1,0:T(4,128)S(1)} %bitcast.664), channel_id=1, source_target_pairs={{4,0},{8,4},{12,8},{16,12},{20,16},{24,20},{28,24},{5,1},{9,5},{13... | collective-permute-start | bytes 3080 | tf_op jit(solution)/shard_map/ppermute | solution.py:24
  44.9 5.3 %collective-permute-start.11 = (f32[2,4,32]{2,1,0:T(4,128)S(1)}, f32[2,4,32]{2,1,0:T(4,128)S(1)}, u32[]{:S(2)}, u32[]{:S(2)}) collective-permute-start(f32[2,4,32]{2,1,0:T(4,128)S(1)} %bitcast.665), channel_id=1, source_target_pairs={{0,4},{4,8},{8,12},{12,16},{16,20},{20,24},{24,28},{1,5},{5,9},{9,... | collective-permute-start | bytes 3080 | tf_op jit(solution)/shard_map/ppermute | solution.py:24
  52.8 3.2 %collective-permute-start.15 = (f32[4,2,4,32]{3,2,0,1:T(4,128)S(1)}, f32[4,2,4,32]{3,2,0,1:T(4,128)S(1)}, u32[]{:S(2)}, u32[]{:S(2)}) collective-permute-start(f32[4,2,4,32]{3,2,0,1:T(4,128)S(1)} %pad_maximum_fusion.6), channel_id=1, source_target_pairs={{0,3},{1,0},{2,1},{3,2},{4,7},{5,4},{6,5},{7,6},{8,11},{9,8},{10,9... | collective-permute-start | bytes 12296 | tf_op jit(solution)/shard_map/ppermute | solution.py:29
  59.1 5.6 %collective-permute-start.17 = (f32[3,4,32]{2,1,0:T(4,128)S(1)}, f32[3,4,32]{2,1,0:T(4,128)S(1)}, u32[]{:S(2)}, u32[]{:S(2)}) collective-permute-start(f32[3,4,32]{2,1,0:T(4,128)S(1)} %bitcast.660), channel_id=1, source_target_pairs={{4,0},{8,4},{12,8},{16,12},{20,16},{24,20},{28,24},{5,1},{9,5},{13... | collective-permute-start | bytes 4616 | tf_op jit(solution)/shard_map/ppermute | solution.py:24
  61.7 5.3 %collective-permute-start.16 = (f32[3,4,32]{2,1,0:T(4,128)S(1)}, f32[3,4,32]{2,1,0:T(4,128)S(1)}, u32[]{:S(2)}, u32[]{:S(2)}) collective-permute-start(f32[3,4,32]{2,1,0:T(4,128)S(1)} %bitcast.657), channel_id=1, source_target_pairs={{0,4},{4,8},{8,12},{12,16},{16,20},{20,24},{24,28},{1,5},{5,9},{9,... | collective-permute-start | bytes 4616 | tf_op jit(solution)/shard_map/ppermute | solution.py:24
  67.0 3.1 %collective-permute-start.18 = (f32[4,3,4,32]{3,2,1,0:T(4,128)S(1)}, f32[4,3,4,32]{3,2,1,0:T(4,128)S(1)}, u32[]{:S(2)}, u32[]{:S(2)}) collective-permute-start(f32[4,3,4,32]{3,2,1,0:T(4,128)S(1)} %pad_maximum_fusion.2), channel_id=1, source_target_pairs={{0,2},{1,3},{2,0},{3,1},{4,6},{5,7},{6,4},{7,5},{8,10},{9,11},{10,... | collective-permute-start | bytes 18440 | tf_op jit(solution)/shard_map/ppermute | solution.py:29
  70.1 3.3 %collective-permute-start.20 = (f32[4,3,4,32]{3,2,1,0:T(4,128)S(1)}, f32[4,3,4,32]{3,2,1,0:T(4,128)S(1)}, u32[]{:S(2)}, u32[]{:S(2)}) collective-permute-start(f32[4,3,4,32]{3,2,1,0:T(4,128)S(1)} %pad_maximum_fusion.2), channel_id=1, source_target_pairs={{0,3},{1,0},{2,1},{3,2},{4,7},{5,4},{6,5},{7,6},{8,11},{9,8},{10,9... | collective-permute-start | bytes 18440 | tf_op jit(solution)/shard_map/ppermute | solution.py:29
  76.0 5.6 %collective-permute-start.22 = (f32[2,4,32]{2,1,0:T(4,128)S(1)}, f32[2,4,32]{2,1,0:T(4,128)S(1)}, u32[]{:S(2)}, u32[]{:S(2)}) collective-permute-start(f32[2,4,32]{2,1,0:T(4,128)S(1)} %bitcast.666), channel_id=1, source_target_pairs={{4,0},{8,4},{12,8},{16,12},{20,16},{24,20},{28,24},{5,1},{9,5},{13... | collective-permute-start | bytes 3080 | tf_op jit(solution)/shard_map/ppermute | solution.py:24
  78.0 5.3 %collective-permute-start.21 = (f32[2,4,32]{2,1,0:T(4,128)S(1)}, f32[2,4,32]{2,1,0:T(4,128)S(1)}, u32[]{:S(2)}, u32[]{:S(2)}) collective-permute-start(f32[2,4,32]{2,1,0:T(4,128)S(1)} %bitcast.668), channel_id=1, source_target_pairs={{0,4},{4,8},{8,12},{12,16},{16,20},{20,24},{24,28},{1,5},{5,9},{9,... | collective-permute-start | bytes 3080 | tf_op jit(solution)/shard_map/ppermute | solution.py:24
  85.3 3.2 %collective-permute-start.25 = (f32[4,2,4,32]{3,2,0,1:T(4,128)S(1)}, f32[4,2,4,32]{3,2,0,1:T(4,128)S(1)}, u32[]{:S(2)}, u32[]{:S(2)}) collective-permute-start(f32[4,2,4,32]{3,2,0,1:T(4,128)S(1)} %pad_maximum_fusion.7), channel_id=1, source_target_pairs={{0,3},{1,0},{2,1},{3,2},{4,7},{5,4},{6,5},{7,6},{8,11},{9,8},{10,9... | collective-permute-start | bytes 12296 | tf_op jit(solution)/shard_map/ppermute | solution.py:29
  91.7 5.6 %collective-permute-start.27 = (f32[3,4,32]{2,1,0:T(4,128)S(1)}, f32[3,4,32]{2,1,0:T(4,128)S(1)}, u32[]{:S(2)}, u32[]{:S(2)}) collective-permute-start(f32[3,4,32]{2,1,0:T(4,128)S(1)} %bitcast.661), channel_id=1, source_target_pairs={{4,0},{8,4},{12,8},{16,12},{20,16},{24,20},{28,24},{5,1},{9,5},{13... | collective-permute-start | bytes 4616 | tf_op jit(solution)/shard_map/ppermute | solution.py:24
  94.3 5.3 %collective-permute-start.26 = (f32[3,4,32]{2,1,0:T(4,128)S(1)}, f32[3,4,32]{2,1,0:T(4,128)S(1)}, u32[]{:S(2)}, u32[]{:S(2)}) collective-permute-start(f32[3,4,32]{2,1,0:T(4,128)S(1)} %bitcast.658), channel_id=1, source_target_pairs={{0,4},{4,8},{8,12},{12,16},{16,20},{20,24},{24,28},{1,5},{5,9},{9,... | collective-permute-start | bytes 4616 | tf_op jit(solution)/shard_map/ppermute | solution.py:24
  99.6 2.9 %collective-permute-start.28 = (f32[4,3,4,32]{3,2,1,0:T(4,128)S(1)}, f32[4,3,4,32]{3,2,1,0:T(4,128)S(1)}, u32[]{:S(2)}, u32[]{:S(2)}) collective-permute-start(f32[4,3,4,32]{3,2,1,0:T(4,128)S(1)} %pad_maximum_fusion.3), channel_id=1, source_target_pairs={{0,2},{1,3},{2,0},{3,1},{4,6},{5,7},{6,4},{7,5},{8,10},{9,11},{10,... | collective-permute-start | bytes 18440 | tf_op jit(solution)/shard_map/ppermute | solution.py:29
  102.5 3.3 %collective-permute-start.30 = (f32[4,3,4,32]{3,2,1,0:T(4,128)S(1)}, f32[4,3,4,32]{3,2,1,0:T(4,128)S(1)}, u32[]{:S(2)}, u32[]{:S(2)}) collective-permute-start(f32[4,3,4,32]{3,2,1,0:T(4,128)S(1)} %pad_maximum_fusion.3), channel_id=1, source_target_pairs={{0,3},{1,0},{2,1},{3,2},{4,7},{5,4},{6,5},{7,6},{8,11},{9,8},{10,9... | collective-permute-start | bytes 18440 | tf_op jit(solution)/shard_map/ppermute | solution.py:29
  108.5 5.6 %collective-permute-start.32 = (f32[2,4,32]{2,1,0:T(4,128)S(1)}, f32[2,4,32]{2,1,0:T(4,128)S(1)}, u32[]{:S(2)}, u32[]{:S(2)}) collective-permute-start(f32[2,4,32]{2,1,0:T(4,128)S(1)} %bitcast.667), channel_id=1, source_target_pairs={{4,0},{8,4},{12,8},{16,12},{20,16},{24,20},{28,24},{5,1},{9,5},{13... | collective-permute-start | bytes 3080 | tf_op jit(solution)/shard_map/ppermute | solution.py:24
  110.4 5.3 %collective-permute-start.31 = (f32[2,4,32]{2,1,0:T(4,128)S(1)}, f32[2,4,32]{2,1,0:T(4,128)S(1)}, u32[]{:S(2)}, u32[]{:S(2)}) collective-permute-start(f32[2,4,32]{2,1,0:T(4,128)S(1)} %bitcast.669), channel_id=1, source_target_pairs={{0,4},{4,8},{8,12},{12,16},{16,20},{20,24},{24,28},{1,5},{5,9},{9,... | collective-permute-start | bytes 3080 | tf_op jit(solution)/shard_map/ppermute | solution.py:24
  117.8 3.2 %collective-permute-start.35 = (f32[4,2,4,32]{3,2,0,1:T(4,128)S(1)}, f32[4,2,4,32]{3,2,0,1:T(4,128)S(1)}, u32[]{:S(2)}, u32[]{:S(2)}) collective-permute-start(f32[4,2,4,32]{3,2,0,1:T(4,128)S(1)} %pad_maximum_fusion.8), channel_id=1, source_target_pairs={{0,3},{1,0},{2,1},{3,2},{4,7},{5,4},{6,5},{7,6},{8,11},{9,8},{10,9... | collective-permute-start | bytes 12296 | tf_op jit(solution)/shard_map/ppermute | solution.py:29
  124.1 5.8 %collective-permute-start.37 = (f32[3,4,32]{2,1,0:T(4,128)S(1)}, f32[3,4,32]{2,1,0:T(4,128)S(1)}, u32[]{:S(2)}, u32[]{:S(2)}) collective-permute-start(f32[3,4,32]{2,1,0:T(4,128)S(1)} %bitcast.663), channel_id=1, source_target_pairs={{4,0},{8,4},{12,8},{16,12},{20,16},{24,20},{28,24},{5,1},{9,5},{13... | collective-permute-start | bytes 4616 | tf_op jit(solution)/shard_map/ppermute | solution.py:24
  126.1 5.3 %collective-permute-start.36 = (f32[3,4,32]{2,1,0:T(4,128)S(1)}, f32[3,4,32]{2,1,0:T(4,128)S(1)}, u32[]{:S(2)}, u32[]{:S(2)}) collective-permute-start(f32[3,4,32]{2,1,0:T(4,128)S(1)} %bitcast.662), channel_id=1, source_target_pairs={{0,4},{4,8},{8,12},{12,16},{16,20},{20,24},{24,28},{1,5},{5,9},{9,... | collective-permute-start | bytes 4616 | tf_op jit(solution)/shard_map/ppermute | solution.py:24
  131.4 3.3 %collective-permute-start.38 = (f32[4,3,4,32]{3,2,1,0:T(4,128)S(1)}, f32[4,3,4,32]{3,2,1,0:T(4,128)S(1)}, u32[]{:S(2)}, u32[]{:S(2)}) collective-permute-start(f32[4,3,4,32]{3,2,1,0:T(4,128)S(1)} %pad_maximum_fusion.4), channel_id=1, source_target_pairs={{0,2},{1,3},{2,0},{3,1},{4,6},{5,7},{6,4},{7,5},{8,10},{9,11},{10,... | collective-permute-start | bytes 18440 | tf_op jit(solution)/shard_map/ppermute | solution.py:29
  134.6 3.3 %collective-permute-start.40 = (f32[4,3,4,32]{3,2,1,0:T(4,128)S(1)}, f32[4,3,4,32]{3,2,1,0:T(4,128)S(1)}, u32[]{:S(2)}, u32[]{:S(2)}) collective-permute-start(f32[4,3,4,32]{3,2,1,0:T(4,128)S(1)} %pad_maximum_fusion.4), channel_id=1, source_target_pairs={{0,3},{1,0},{2,1},{3,2},{4,7},{5,4},{6,5},{7,6},{8,11},{9,8},{10,9... | collective-permute-start | bytes 18440 | tf_op jit(solution)/shard_map/ppermute | solution.py:29
  140.9 5.6 %collective-permute-start.41 = (f32[3,4,1024]{2,0,1:T(4,128)S(1)}, f32[3,4,1024]{2,0,1:T(4,128)S(1)}, u32[]{:S(2)}, u32[]{:S(2)}) collective-permute-start(f32[3,4,1024]{2,0,1:T(4,128)S(1)} %slice.1071), channel_id=1, source_target_pairs={{1,0},{2,1},{3,2},{5,4},{6,5},{7,6},{9,8},{10,9},{11,10},{13,12},{... | collective-permute-start | bytes 147464 | tf_op jit(solution)/shard_map/ppermute | solution.py:24
  (20 other events, 42.7 us)
where the time goes:
time: 149 us; the launch traced here: 148 us
  starting transfers between devices  67.2 us (45%)
  waiting for transfers between devices  40.9 us (27%)
  local copies, waits for them, and re-layouts  27.2 us (18%)
  other arithmetic  9.08 us (6%)
  between operations  3.27 us (2%)
    ppermute x18, starting transfers between devices, from_behind(): lax.ppermute(value, axis, [(source, source + steps) for source in range(l...  48.1 us
    ppermute x24, waiting for transfers between devices, passed_along(): lax.ppermute(x, axis, [(i, (i + by) % devices) for i in range(devices)])  25.3 us
    ppermute x24, starting transfers between devices, passed_along(): lax.ppermute(x, axis, [(i, (i + by) % devices) for i in range(devices)])  19.1 us
    ppermute x18, waiting for transfers between devices, from_behind(): lax.ppermute(value, axis, [(source, source + steps) for source in range(l...  15.7 us
    unnamed x68, local copies, waits for them, and re-layouts  6.64 us
    gather x16, local copies, waits for them, and re-layouts, edge_halos(): fetched = jnp.take(assembled, window_index, axis=1)  4.74 us
  transfers between devices with their start and end apart: 42, of which 26 were waited for; matrix products, arithmetic and copies ran while one was open for 9% of the time, Pallas kernels for 0%

commit v1 on v0

v1 whole, which is shorter than its diff:
```python
import jax
import jax.numpy as jnp
from jax import lax
from jax.experimental import pallas as pl
from jax.experimental.pallas import tpu as pltpu
from jax.sharding import PartitionSpec as P

SUBCYCLES = 4
RELAX_RATE = 0.8
STEP_WEIGHT = 0.5
AIR_DRAG = 0.3
WATER_DRAG = 0.6
TOPMOST_WARMTH = -12.0
FREEZING = -1.8
DIFFUSION = 0.6
THERMAL_KAPPA = 0.1
OPEN_HEAT = 0.4
OPEN_WIND = 0.5

EDGE = 32
TILE = 4
MESH = pl.DeviceIdType.MESH


def lanes():
    return lax.broadcasted_iota(jnp.int32, (8, 128), 1)


def swap_groups(a, b, width, low):
    return (
        jnp.where(low, a, pltpu.roll(b, width, 1)),
        jnp.where(low, pltpu.roll(a, 128 - width, 1), b),
    )


def transpose4(parts):
    lane = lanes()
    low64 = lane < 64
    low32 = (lane % 64) < 32
    a, b, c, d = parts
    a, c = swap_groups(a, c, 64, low64)
    b, d = swap_groups(b, d, 64, low64)
    a, b = swap_groups(a, b, 32, low32)
    c, d = swap_groups(c, d, 32, low32)
    return [a, b, c, d]


def pick(parts, index):
    value = parts[0]
    for i in range(1, len(parts)):
        value = jnp.where(index == i, parts[i], value)
    return value


def solve_layers(warm_ref, out_ref, weight, surface, alive):
    layers = warm_ref.shape[0]
    thickness = weight * (1.0 / 0.9)
    inverse = 1.0 / thickness
    c = DIFFUSION * inverse * inverse
    diagonal = 1.0 + 2.0 * c
    ratios, partial = [], []
    for l in range(layers):
        supply = warm_ref[l, 0]
        if l == 0:
            supply = supply + c * TOPMOST_WARMTH
        if l == layers - 1:
            supply = supply + c * surface
        if l == 0:
            pivot = diagonal
        else:
            pivot = diagonal - c * ratios[-1]
            supply = supply + c * partial[-1]
        flip = 1.0 / pivot
        partial.append(supply * flip)
        ratios.append(c * flip)
    value = partial[-1]
    flux = THERMAL_KAPPA * (value - surface) * inverse
    out_ref[layers - 1, 0] = jnp.where(alive, value, 0.0)
    for l in range(layers - 2, -1, -1):
        value = partial[l] + ratios[l] * value
        out_ref[l, 0] = jnp.where(alive, value, 0.0)
    return flux


def kernel(
    rows,
    cols,
    skin, motion, tensor, weight, strength, warm, filled, flags, source,
    motion_out, tensor_out, warm_out, ocean_out,
    B, TS, TSS, HF, F, K, KS, G, D, DS, send, recv,
):
    me_r = lax.axis_index("row")
    me_c = lax.axis_index("col")
    east = (me_r, lax.rem(me_c + 1, cols))
    west = (me_r, lax.rem(me_c + cols - 1, cols))
    north = (me_r + 1, me_c)
    south = (me_r - 1, me_c)
    has_north = me_r < rows - 1
    has_south = me_r > 0

    F[:, :, 8:16, :] = jnp.zeros((9, 4, 8, 128), jnp.float32)
    K[:, :, 8:16, :] = jnp.zeros((2, 4, 8, 128), jnp.float32)

    barrier = pltpu.get_barrier_semaphore()
    pl.semaphore_signal(barrier, inc=1, device_id=east, device_id_type=MESH)
    pl.semaphore_signal(barrier, inc=1, device_id=west, device_id_type=MESH)

    @pl.when(has_north)
    def _():
        pl.semaphore_signal(barrier, inc=1, device_id=north, device_id_type=MESH)

    @pl.when(has_south)
    def _():
        pl.semaphore_signal(barrier, inc=1, device_id=south, device_id_type=MESH)

    first = me_c * TILE
    block_index, block_covered = [], []
    out_rank = jnp.int32(0)
    out_first = jnp.int32(0)
    out_second = jnp.int32(0)
    for b in range(TILE):
        own = jnp.int32(-1)
        for j in range(TILE):
            own = jnp.where(source[0, j] == first + b, j, own)
        covered = flags[0, b] == 1
        moved = jnp.logical_and(covered, own < 0)
        block_index.append(jnp.where(own >= 0, own, TILE + jnp.minimum(out_rank, 1)))
        block_covered.append(covered)
        out_first = jnp.where(jnp.logical_and(moved, out_rank == 0), b, out_first)
        out_second = jnp.where(jnp.logical_and(moved, out_rank == 1), b, out_second)
        out_rank = out_rank + jnp.where(moved, 1, 0)
    slot_index = [
        jnp.where(source[0, j] >= first, jnp.minimum(source[0, j] - first, TILE - 1), TILE + min(j, 1))
        for j in range(TILE)
    ]

    for f in range(2):
        B[0:4, f] = motion[f, 0].reshape(4, 8, 128)
    for f in range(3):
        B[0:4, 2 + f] = tensor[f, 0].reshape(4, 8, 128)
    B[0:4, 5] = weight[0].reshape(4, 8, 128)
    B[0:4, 6] = strength[0].reshape(4, 8, 128)

    surface = transpose4([skin[0, pl.ds(q, 8, stride=4), :] for q in range(4)])
    for b in range(4):
        TS[b] = surface[b]
    TSS[0] = pick(surface, out_first)
    TSS[1] = pick(surface, out_second)

    peers = 2 + jnp.minimum(me_r, 1) + jnp.minimum(rows - 1 - me_r, 1)
    pl.semaphore_wait(barrier, peers)

    def remote(k, src, dst, device):
        return pltpu.make_async_remote_copy(
            src_ref=src, dst_ref=dst, send_sem=send.at[k], recv_sem=recv.at[k],
            device_id=device, device_id_type=MESH,
        )

    slots_west = remote(0, B.at[0:2], B.at[4:6], west)
    slots_west.start()
    temps_east = remote(1, TSS, TS.at[4:6], east)
    temps_east.start()

    for q in range(4):
        at = pl.ds(q, 8, stride=4)
        F[7, q, 0:8] = AIR_DRAG * skin[3, at, :] + WATER_DRAG * skin[1, at, :]
        F[8, q, 0:8] = AIR_DRAG * skin[4, at, :] + WATER_DRAG * skin[2, at, :]

    slots_west.wait_recv()
    group = lanes() // 8
    pack_e = [jnp.zeros((8, 128), jnp.float32)] * 4
    pack_w = [jnp.zeros((8, 128), jnp.float32)] * 4
    for p in range(9):
        if p < 7:
            held = [
                jnp.where(block_covered[b], B[block_index[b], p], 0.0) for b in range(4)
            ]
            held = transpose4(held)
        for q in range(4):
            if p < 7:
                F[p, q, 0:8] = held[q]
                value = held[q]
            else:
                value = F[p, q, 0:8]
            turned = pltpu.roll(value, 8 * p, 1) if p else value
            pack_e[q] = jnp.where(group == p, turned, pack_e[q])
            pack_w[q] = jnp.where(group == (p + 15) % 16, turned, pack_w[q])
    for q in range(4):
        KS[0, q] = pack_e[q]
        KS[1, q] = pack_w[q]

    strip_west = remote(2, KS.at[0], K.at[0, :, 0:8, :], west)
    strip_east = remote(3, KS.at[1], K.at[1, :, 0:8, :], east)
    strip_west.start()
    strip_east.start()
    rows_north = remote(4, F.at[:, :, 6:8, :], F.at[:, :, 14:16, :], north)
    rows_south = remote(5, F.at[:, :, 0:2, :], F.at[:, :, 8:10, :], south)
    corner_north = remote(6, K.at[:, :, 6:8, :], K.at[:, :, 14:16, :], north)
    corner_south = remote(7, K.at[:, :, 0:2, :], K.at[:, :, 8:10, :], south)

    @pl.when(has_north)
    def _():
        rows_north.start()

    @pl.when(has_south)
    def _():
        rows_south.start()

    temps_east.wait_recv()
    slot_row = lax.broadcasted_iota(jnp.int32, (4, 1024), 0)
    alive = slot_row < filled[0, 0]
    slot_surface = jnp.stack([TS[slot_index[j]] for j in range(4)]).reshape(4, 1024)
    flux = solve_layers(warm, warm_out, weight[0], slot_surface, alive)
    HF[0:4] = flux.reshape(4, 8, 128)
    heat_west = remote(8, HF.at[0:2], HF.at[4:6], west)
    heat_west.start()

    strip_west.wait_recv()
    strip_east.wait_recv()

    @pl.when(has_north)
    def _():
        corner_north.start()

    @pl.when(has_south)
    def _():
        corner_south.start()

    @pl.when(has_south)
    def _():
        rows_north.wait_recv()

    @pl.when(has_north)
    def _():
        rows_south.wait_recv()

    @pl.when(has_south)
    def _():
        corner_north.wait_recv()

    @pl.when(has_north)
    def _():
        corner_south.wait_recv()

    wide = lax.broadcasted_iota(jnp.int32, (16, 128), 1) // 8
    for q in range(4):
        from_e = K[0, q]
        from_w = K[1, q]
        planes = []
        for p in range(9):
            side = jnp.where(wide == p, from_e, jnp.where(wide == (p + 15) % 16, from_w, 0.0))
            if p:
                side = pltpu.roll(side, 128 - 8 * p, 1)
            planes.append(jnp.concatenate([F[p, q], side], axis=1))
        for p in range(5):
            G[p, q] = planes[p]
        mass = planes[5]
        icy = mass > 0.0
        flip = jnp.where(icy, 1.0 / (mass + STEP_WEIGHT * WATER_DRAG), 0.0)
        G[5, q] = mass * flip
        G[6, q] = (0.5 * STEP_WEIGHT) * flip
        G[7, q] = planes[6]
        G[8, q] = STEP_WEIGHT * flip * planes[7]
        G[9, q] = STEP_WEIGHT * flip * planes[8]

    def across_x(x):
        return pltpu.roll(x, 255, 1) - pltpu.roll(x, 1, 1)

    def across_y(p, q):
        upper = G[p, q + 1] if q < 3 else pltpu.roll(G[p, 0], 15, 0)
        lower = G[p, q - 1] if q > 0 else pltpu.roll(G[p, 3], 1, 0)
        return upper - lower

    keep = 1.0 / (1.0 + RELAX_RATE)
    mix = RELAX_RATE / (1.0 + RELAX_RATE)

    def subcycle(step, carry):
        for q in range(4):
            ux = across_x(G[0, q])
            vx = across_x(G[1, q])
            uy = across_y(0, q)
            vy = across_y(1, q)
            power = G[7, q]
            divergence = 0.5 * (ux + vy)
            tension = 0.5 * (ux - vy)
            shearing = 0.25 * (uy + vx)
            square = (
                divergence * divergence
                + 0.25 * (tension * tension + 4.0 * shearing * shearing)
                + 0.25
            )
            viscosity = (0.5 * mix) * power * lax.rsqrt(square)
            common = 0.75 * viscosity * divergence - (0.25 * mix) * power
            half = 0.25 * viscosity
            G[2, q] = keep * G[2, q] + half * ux + common
            G[3, q] = keep * G[3, q] + half * vy + common
            G[4, q] = keep * G[4, q] + 0.5 * viscosity * shearing
        for q in range(4):
            force_e = across_x(G[2, q]) + across_y(4, q)
            force_n = across_x(G[4, q]) + across_y(3, q)
            share = G[6, q]
            stay = G[5, q]
            G[0, q] = stay * G[0, q] + share * force_e + G[8, q]
            G[1, q] = stay * G[1, q] + share * force_n + G[9, q]
        return carry

    lax.fori_loop(0, SUBCYCLES, subcycle, 0)

    for p in range(5):
        blocks = transpose4([G[p, q, 0:8, 0:128] for q in range(4)])
        for b in range(4):
            D[b, p] = blocks[b]
        DS[0, p] = pick(blocks, out_first)
        DS[1, p] = pick(blocks, out_second)
    back_east = remote(9, DS, D.at[4:6], east)
    back_east.start()

    heat_west.wait_recv()
    lane_block = lanes() // EDGE
    ice = jnp.zeros((8, 128), jnp.int32)
    for b in range(4):
        ice = jnp.where(lane_block == b, jnp.where(block_covered[b], 1, 0), ice)
    ice = ice == 1
    heat = transpose4([HF[block_index[b]] for b in range(4)])
    for q in range(4):
        at = pl.ds(q, 8, stride=4)
        ocean_out[0, at, :] = jnp.where(ice, heat[q], -OPEN_HEAT * (skin[0, at, :] - FREEZING))
        for f in range(2):
            ocean_out[1 + f, at, :] = jnp.where(
                ice,
                WATER_DRAG * (G[f, q, 0:8, 0:128] - skin[1 + f, at, :]),
                OPEN_WIND * skin[3 + f, at, :],
            )

    back_east.wait_recv()
    for p in range(5):
        value = jnp.stack([D[slot_index[j], p] for j in range(4)]).reshape(4, 1024)
        value = jnp.where(alive, value, 0.0)
        if p < 2:
            motion_out[p, 0] = value
        else:
            tensor_out[p - 2, 0] = value

    for copy in (slots_west, temps_east, strip_west, strip_east, heat_west, back_east):
        copy.wait_send()

    @pl.when(has_north)
    def _():
        rows_north.wait_send()
        corner_north.wait_send()

    @pl.when(has_south)
    def _():
        rows_south.wait_send()
        corner_south.wait_send()


def solution(mesh):
    rows, cols = mesh.shape["row"], mesh.shape["col"]

    def local(skin, motion, tensor, weight, strength, warm, filled, flags, source, adjacent):
        vmem = pl.BlockSpec(memory_space=pltpu.VMEM)
        smem = pl.BlockSpec(memory_space=pltpu.SMEM)
        f32 = jnp.float32

        def body(*refs):
            kernel(rows, cols, *refs)

        return pl.pallas_call(
            body,
            out_shape=tuple(
                jax.ShapeDtypeStruct(s, f32)
                for s in (motion.shape, tensor.shape, warm.shape, (3,) + skin.shape[1:])
            ),
            in_specs=[vmem] * 6 + [smem] * 3,
            out_specs=(vmem,) * 4,
            scratch_shapes=[
                pltpu.VMEM((6, 7, 8, 128), f32),
                pltpu.VMEM((6, 8, 128), f32),
                pltpu.VMEM((2, 8, 128), f32),
                pltpu.VMEM((6, 8, 128), f32),
                pltpu.VMEM((9, 4, 16, 128), f32),
                pltpu.VMEM((2, 4, 16, 128), f32),
                pltpu.VMEM((2, 4, 8, 128), f32),
                pltpu.VMEM((10, 4, 16, 256), f32),
                pltpu.VMEM((6, 5, 8, 128), f32),
                pltpu.VMEM((2, 5, 8, 128), f32),
                pltpu.SemaphoreType.DMA((10,)),
                pltpu.SemaphoreType.DMA((10,)),
            ],
            compiler_params=pltpu.CompilerParams(
                collective_id=0, has_side_effects=True, vmem_limit_bytes=16 * 1024 * 1024
            ),
        )(skin, motion, tensor, weight, strength, warm, filled, flags, source)

    in_specs = (
        P(None, "row", "col"),
        P(None, "row", "col", None),
        P(None, "row", "col", None),
        P("row", "col", None),
        P("row", "col", None),
        P(None, "row", "col"),
        P("row", "col"),
        P("row", "col"),
        P("row", "col"),
        P(None, "row", "col"),
    )
    out_specs = (
        P(None, "row", "col", None),
        P(None, "row", "col", None),
        P(None, "row", "col", None),
        P(None, "row", "col"),
    )
    return jax.shard_map(local, mesh=mesh, in_specs=in_specs, out_specs=out_specs, check_vma=False)
```

time: 149 us -> 23.7 us (0.16)
  the two profiles are of different devices: /device:TPU:25 before, /device:TPU:0 now
where the time goes in v1:
time: 23.7 us; the launch traced here: 23.3 us
  Pallas kernels  14.7 us (62%)
  local copies, waits for them, and re-layouts  7.28 us (31%)
  between operations  1.35 us (6%)
    pallas_call x1, Pallas kernels, local(): pl.pallas_call(body, out_shape=tuple((jax.ShapeDtypeStruct(s, f32) for s...  14.7 us
    unnamed x20, local copies, waits for them, and re-layouts  7.28 us

profile of v1, /device:TPU:0, one launch (start us, length us, event | category | flops | bytes accessed | tf_op | source)
XLA Modules:
  0.0 23.3 jit_solution(539469849667724431)
XLA Ops:
  0.6 0.0 copy-start.7
  0.6 0.0 copy-start.6
  1.3 0.0 copy-done.7
  1.3 0.0 copy-done.6
  1.3 0.0 copy-start
  1.3 0.9 %copy-done = f32[7,1,4,1024]{3,2,1,0:T(4,128)S(1)} copy-done((f32[7,1,4,1024]{3,2,1,0:T(4,128)S(1)}, f32[7,1,4,1024]{3,2,1,0:T(4,128)}, u32[]{:S(2)}) %copy-start) | copy-done | bytes 114712
  2.2 0.0 copy-start.1
  2.2 0.9 %copy-done.1 = f32[5,32,128]{2,1,0:T(8,128)S(1)} copy-done((f32[5,32,128]{2,1,0:T(8,128)S(1)}, f32[5,32,128]{2,1,0:T(8,128)}, u32[]{:S(2)}) %copy-start.1) | copy-done | bytes 81944
  3.1 0.0 copy-start.2
  3.1 0.8 %copy-done.2 = f32[3,1,4,1024]{3,2,1,0:T(4,128)S(1)} copy-done((f32[3,1,4,1024]{3,2,1,0:T(4,128)S(1)}, f32[3,1,4,1024]{3,2,1,0:T(4,128)}, u32[]{:S(2)}) %copy-start.2) | copy-done | bytes 49176
  3.9 0.0 copy-start.3
  3.9 0.8 %copy-done.3 = f32[2,1,4,1024]{3,2,1,0:T(4,128)S(1)} copy-done((f32[2,1,4,1024]{3,2,1,0:T(4,128)S(1)}, f32[2,1,4,1024]{3,2,1,0:T(4,128)}, u32[]{:S(2)}) %copy-start.3) | copy-done | bytes 32792
  4.7 0.0 copy-start.4
  4.7 0.7 %copy-done.4 = f32[1,4,1024]{2,1,0:T(4,128)S(1)} copy-done((f32[1,4,1024]{2,1,0:T(4,128)S(1)}, f32[1,4,1024]{2,1,0:T(4,128)}, u32[]{:S(2)}) %copy-start.4) | copy-done | bytes 16408
  5.4 0.0 copy-start.5
  5.4 0.7 %copy-done.5 = f32[1,4,1024]{2,1,0:T(4,128)S(1)} copy-done((f32[1,4,1024]{2,1,0:T(4,128)S(1)}, f32[1,4,1024]{2,1,0:T(4,128)}, u32[]{:S(2)}) %copy-start.5) | copy-done | bytes 16408
  6.1 14.7 %shard_map.120 = (f32[2,1,4,1024]{3,2,1,0:T(4,128)S(1)}, f32[3,1,4,1024]{3,2,1,0:T(4,128)S(1)}, f32[7,1,4,1024]{3,2,1,0:T(4,128)S(1)}, f32[3,32,128]{2,1,0:T(8,128)S(1)}) custom-call(f32[5,32,128]{2,1,0:T(8,128)S(1)} %copy-done.1, f32[2,1,4,1024]{3,2,1,0:T(4,128)S(1)} %copy-done.3, f32[3,1,4,1024]{3,2,1,0:T(4,128)S(1)} %copy-done.2, ...), custom_call_target="tpu_custom_call" | custom-call | tf_op jit(solution)/shard_map/pallas_call | solution.py:369
  20.8 0.6 %copy.18 = f32[2,1,4,1024]{3,2,1,0:T(4,128)} copy(f32[2,1,4,1024]{3,2,1,0:T(4,128)S(1)} %get-tuple-element.8) | data formatting | bytes 65536
  21.4 0.6 %copy.19 = f32[3,1,4,1024]{3,2,1,0:T(4,128)} copy(f32[3,1,4,1024]{3,2,1,0:T(4,128)S(1)} %get-tuple-element.9) | data formatting | bytes 98304
  22.0 0.6 %copy.20 = f32[7,1,4,1024]{3,2,1,0:T(4,128)} copy(f32[7,1,4,1024]{3,2,1,0:T(4,128)S(1)} %get-tuple-element.10) | data formatting | bytes 229376
  22.7 0.6 %copy.21 = f32[3,32,128]{2,1,0:T(8,128)} copy(f32[3,32,128]{2,1,0:T(8,128)S(1)} %get-tuple-element.11) | data formatting | bytes 98304
Async XLA Ops:
  0.6 0.7 %copy-start.7 = (s32[1,4]{1,0:T(1,128)S(1)}, s32[1,4]{1,0:T(1,128)}, u32[]{:S(2)}) copy-start(s32[1,4]{1,0:T(1,128)} %refs_8_.1) | copy-start | bytes 52
  0.6 0.7 %copy-start.6 = (s32[1,4]{1,0:T(1,128)S(1)}, s32[1,4]{1,0:T(1,128)}, u32[]{:S(2)}) copy-start(s32[1,4]{1,0:T(1,128)} %refs_7_.1) | copy-start | bytes 52
  1.3 0.9 %copy-start = (f32[7,1,4,1024]{3,2,1,0:T(4,128)S(1)}, f32[7,1,4,1024]{3,2,1,0:T(4,128)}, u32[]{:S(2)}) copy-start(f32[7,1,4,1024]{3,2,1,0:T(4,128)} %refs_5_.1) | copy-start | bytes 344068
  2.2 0.9 %copy-start.1 = (f32[5,32,128]{2,1,0:T(8,128)S(1)}, f32[5,32,128]{2,1,0:T(8,128)}, u32[]{:S(2)}) copy-start(f32[5,32,128]{2,1,0:T(8,128)} %refs_0_.1) | copy-start | bytes 245764
  3.1 0.8 %copy-start.2 = (f32[3,1,4,1024]{3,2,1,0:T(4,128)S(1)}, f32[3,1,4,1024]{3,2,1,0:T(4,128)}, u32[]{:S(2)}) copy-start(f32[3,1,4,1024]{3,2,1,0:T(4,128)} %refs_2_.1) | copy-start | bytes 147460
  3.9 0.8 %copy-start.3 = (f32[2,1,4,1024]{3,2,1,0:T(4,128)S(1)}, f32[2,1,4,1024]{3,2,1,0:T(4,128)}, u32[]{:S(2)}) copy-start(f32[2,1,4,1024]{3,2,1,0:T(4,128)} %refs_1_.1) | copy-start | bytes 98308
  4.7 0.7 %copy-start.4 = (f32[1,4,1024]{2,1,0:T(4,128)S(1)}, f32[1,4,1024]{2,1,0:T(4,128)}, u32[]{:S(2)}) copy-start(f32[1,4,1024]{2,1,0:T(4,128)} %refs_3_.1) | copy-start | bytes 49156
  5.4 0.7 %copy-start.5 = (f32[1,4,1024]{2,1,0:T(4,128)S(1)}, f32[1,4,1024]{2,1,0:T(4,128)}, u32[]{:S(2)}) copy-start(f32[1,4,1024]{2,1,0:T(4,128)} %refs_4_.1) | copy-start | bytes 49156

commit v2 on v1

--- a/solution.py
+++ b/solution.py
@@ -85,10 +85,19 @@
 def kernel(
     rows,
     cols,
-    skin, motion, tensor, weight, strength, warm, filled, flags, source,
+    skin_in, motion_in, tensor_in, weight_in, strength_in, warm_in, flags_in, source_in,
     motion_out, tensor_out, warm_out, ocean_out,
     B, TS, TSS, HF, F, K, KS, G, D, DS, send, recv,
+    skin, motion, tensor, weight, strength, warm, flags, source, loaded,
 ):
+    pairs = (
+        (motion_in, motion), (tensor_in, tensor), (weight_in, weight), (strength_in, strength),
+        (skin_in, skin), (source_in, source), (flags_in, flags), (warm_in, warm),
+    )
+    loads = [pltpu.make_async_copy(a, b, loaded.at[i]) for i, (a, b) in enumerate(pairs)]
+    for load in loads:
+        load.start()
+
     me_r = lax.axis_index("row")
     me_c = lax.axis_index("col")
     east = (me_r, lax.rem(me_c + 1, cols))
@@ -97,6 +106,8 @@
     south = (me_r - 1, me_c)
     has_north = me_r < rows - 1
     has_south = me_r > 0
+    diagonal_north = ((me_r + 1, west[1]), (me_r + 1, east[1]))
+    diagonal_south = ((me_r - 1, west[1]), (me_r - 1, east[1]))
 
     F[:, :, 8:16, :] = jnp.zeros((9, 4, 8, 128), jnp.float32)
     K[:, :, 8:16, :] = jnp.zeros((2, 4, 8, 128), jnp.float32)
@@ -107,11 +118,16 @@
 
     @pl.when(has_north)
     def _():
-        pl.semaphore_signal(barrier, inc=1, device_id=north, device_id_type=MESH)
+        for device in (north, *diagonal_north):
+            pl.semaphore_signal(barrier, inc=1, device_id=device, device_id_type=MESH)
 
     @pl.when(has_south)
     def _():
-        pl.semaphore_signal(barrier, inc=1, device_id=south, device_id_type=MESH)
+        for device in (south, *diagonal_south):
+            pl.semaphore_signal(barrier, inc=1, device_id=device, device_id_type=MESH)
+
+    for load in loads[4:7]:
+        load.wait()
 
     first = me_c * TILE
     block_index, block_covered = [], []
@@ -134,6 +150,8 @@
         for j in range(TILE)
     ]
 
+    for load in loads[:4]:
+        load.wait()
     for f in range(2):
         B[0:4, f] = motion[f, 0].reshape(4, 8, 128)
     for f in range(3):
@@ -147,7 +165,7 @@
     TSS[0] = pick(surface, out_first)
     TSS[1] = pick(surface, out_second)
 
-    peers = 2 + jnp.minimum(me_r, 1) + jnp.minimum(rows - 1 - me_r, 1)
+    peers = 2 + 3 * jnp.minimum(me_r, 1) + 3 * jnp.minimum(rows - 1 - me_r, 1)
     pl.semaphore_wait(barrier, peers)
 
     def remote(k, src, dst, device):
@@ -167,80 +185,85 @@
         F[8, q, 0:8] = AIR_DRAG * skin[4, at, :] + WATER_DRAG * skin[2, at, :]
 
     slots_west.wait_recv()
+    for p in range(7):
+        held = [jnp.where(block_covered[b], B[block_index[b], p], 0.0) for b in range(4)]
+        held = transpose4(held)
+        for q in range(4):
+            F[p, q, 0:8] = held[q]
+
+    rows_north = remote(4, F.at[:, :, 6:8, :], F.at[:, :, 14:16, :], north)
+    rows_south = remote(5, F.at[:, :, 0:2, :], F.at[:, :, 8:10, :], south)
+
+    @pl.when(has_north)
+    def _():
+        rows_north.start()
+
+    @pl.when(has_south)
+    def _():
+        rows_south.start()
+
     group = lanes() // 8
-    pack_e = [jnp.zeros((8, 128), jnp.float32)] * 4
-    pack_w = [jnp.zeros((8, 128), jnp.float32)] * 4
-    for p in range(9):
-        if p < 7:
-            held = [
-                jnp.where(block_covered[b], B[block_index[b], p], 0.0) for b in range(4)
-            ]
-            held = transpose4(held)
-        for q in range(4):
-            if p < 7:
-                F[p, q, 0:8] = held[q]
-                value = held[q]
-            else:
-                value = F[p, q, 0:8]
-            turned = pltpu.roll(value, 8 * p, 1) if p else value
-            pack_e[q] = jnp.where(group == p, turned, pack_e[q])
-            pack_w[q] = jnp.where(group == (p + 15) % 16, turned, pack_w[q])
     for q in range(4):
-        KS[0, q] = pack_e[q]
-        KS[1, q] = pack_w[q]
+        pack_e = jnp.zeros((8, 128), jnp.float32)
+        pack_w = jnp.zeros((8, 128), jnp.float32)
+        for p in range(9):
+            turned = F[p, q, 0:8]
+            if p:
+                turned = pltpu.roll(turned, 8 * p, 1)
+            pack_e = jnp.where(group == p, turned, pack_e)
+            pack_w = jnp.where(group == (p + 15) % 16, turned, pack_w)
+        KS[0, q] = pack_e
+        KS[1, q] = pack_w
+
+    corners_north = [
+        remote(6 + 2 * i, KS.at[i, :, 6:8, :], K.at[i, :, 14:16, :], diagonal_north[i])
+        for i in range(2)
+    ]
+    corners_south = [
+        remote(7 + 2 * i, KS.at[i, :, 0:2, :], K.at[i, :, 8:10, :], diagonal_south[i])
+        for i in range(2)
+    ]
+
+    @pl.when(has_north)
+    def _():
+        for corner in corners_north:
+            corner.start()
+
+    @pl.when(has_south)
+    def _():
+        for corner in corners_south:
+            corner.start()
 
     strip_west = remote(2, KS.at[0], K.at[0, :, 0:8, :], west)
     strip_east = remote(3, KS.at[1], K.at[1, :, 0:8, :], east)
     strip_west.start()
     strip_east.start()
-    rows_north = remote(4, F.at[:, :, 6:8, :], F.at[:, :, 14:16, :], north)
-    rows_south = remote(5, F.at[:, :, 0:2, :], F.at[:, :, 8:10, :], south)
-    corner_north = remote(6, K.at[:, :, 6:8, :], K.at[:, :, 14:16, :], north)
-    corner_south = remote(7, K.at[:, :, 0:2, :], K.at[:, :, 8:10, :], south)
-
-    @pl.when(has_north)
-    def _():
-        rows_north.start()
-
-    @pl.when(has_south)
-    def _():
-        rows_south.start()
 
     temps_east.wait_recv()
+    loads[7].wait()
     slot_row = lax.broadcasted_iota(jnp.int32, (4, 1024), 0)
-    alive = slot_row < filled[0, 0]
+    alive_rows = jnp.zeros((4, 1024), jnp.int32)
+    for j in range(TILE):
+        alive_rows = jnp.where(slot_row == j, source[0, j], alive_rows)
+    alive = alive_rows >= 0
     slot_surface = jnp.stack([TS[slot_index[j]] for j in range(4)]).reshape(4, 1024)
     flux = solve_layers(warm, warm_out, weight[0], slot_surface, alive)
     HF[0:4] = flux.reshape(4, 8, 128)
-    heat_west = remote(8, HF.at[0:2], HF.at[4:6], west)
+    heat_west = remote(10, HF.at[0:2], HF.at[4:6], west)
     heat_west.start()
 
     strip_west.wait_recv()
     strip_east.wait_recv()
 
+    @pl.when(has_south)
+    def _():
+        for copy in (rows_north, *corners_north):
+            copy.wait_recv()
+
     @pl.when(has_north)
     def _():
-        corner_north.start()
-
-    @pl.when(has_south)
-    def _():
-        corner_south.start()
-
-    @pl.when(has_south)
-    def _():
-        rows_north.wait_recv()
-
-    @pl.when(has_north)
-    def _():
-        rows_south.wait_recv()
-
-    @pl.when(has_south)
-    def _():
-        corner_north.wait_recv()
-
-    @pl.when(has_north)
-    def _():
-        corner_south.wait_recv()
+        for copy in (rows_south, *corners_south):
+            copy.wait_recv()
 
     wide = lax.broadcasted_iota(jnp.int32, (16, 128), 1) // 8
     for q in range(4):
@@ -312,7 +335,7 @@
             D[b, p] = blocks[b]
         DS[0, p] = pick(blocks, out_first)
         DS[1, p] = pick(blocks, out_second)
-    back_east = remote(9, DS, D.at[4:6], east)
+    back_east = remote(11, DS, D.at[4:6], east)
     back_east.start()
 
     heat_west.wait_recv()
@@ -346,13 +369,13 @@
 
     @pl.when(has_north)
     def _():
-        rows_north.wait_send()
-        corner_north.wait_send()
+        for copy in (rows_north, *corners_north):
+            copy.wait_send()
 
     @pl.when(has_south)
     def _():
-        rows_south.wait_send()
-        corner_south.wait_send()
+        for copy in (rows_south, *corners_south):
+            copy.wait_send()
 
 
 def solution(mesh):
@@ -360,19 +383,21 @@
 
     def local(skin, motion, tensor, weight, strength, warm, filled, flags, source, adjacent):
         vmem = pl.BlockSpec(memory_space=pltpu.VMEM)
-        smem = pl.BlockSpec(memory_space=pltpu.SMEM)
+        hbm = pl.BlockSpec(memory_space=pltpu.HBM)
         f32 = jnp.float32
+        arguments = (skin, motion, tensor, weight, strength, warm, flags, source)
 
         def body(*refs):
             kernel(rows, cols, *refs)
 
-        return pl.pallas_call(
+        out_shape = tuple(
+            jax.ShapeDtypeStruct(s, f32)
+            for s in (motion.shape, tensor.shape, warm.shape, (3,) + skin.shape[1:])
+        )
+        results = pl.pallas_call(
             body,
-            out_shape=tuple(
-                jax.ShapeDtypeStruct(s, f32)
-                for s in (motion.shape, tensor.shape, warm.shape, (3,) + skin.shape[1:])
-            ),
-            in_specs=[vmem] * 6 + [smem] * 3,
+            out_shape=out_shape,
+            in_specs=[hbm] * 8,
             out_specs=(vmem,) * 4,
             scratch_shapes=[
                 pltpu.VMEM((6, 7, 8, 128), f32),
@@ -385,13 +410,17 @@
                 pltpu.VMEM((10, 4, 16, 256), f32),
                 pltpu.VMEM((6, 5, 8, 128), f32),
                 pltpu.VMEM((2, 5, 8, 128), f32),
-                pltpu.SemaphoreType.DMA((10,)),
-                pltpu.SemaphoreType.DMA((10,)),
+                pltpu.SemaphoreType.DMA((12,)),
+                pltpu.SemaphoreType.DMA((12,)),
+                *(pltpu.VMEM(a.shape, f32) for a in (skin, motion, tensor, weight, strength, warm)),
+                *(pltpu.SMEM(a.shape, jnp.int32) for a in (flags, source)),
+                pltpu.SemaphoreType.DMA((8,)),
             ],
             compiler_params=pltpu.CompilerParams(
-                collective_id=0, has_side_effects=True, vmem_limit_bytes=16 * 1024 * 1024
+                collective_id=0, has_side_effects=True, vmem_limit_bytes=32 * 1024 * 1024
             ),
-        )(skin, motion, tensor, weight, strength, warm, filled, flags, source)
+        )(*(pltpu.with_memory_space_constraint(a, pltpu.HBM) for a in arguments))
+        return results
 
     in_specs = (
         P(None, "row", "col"),

time: 23.7 us -> 17.2 us (0.73)
  local copies, waits for them, and re-layouts: 7.28 us -> 2.5 us
  Pallas kernels: 14.7 us -> 13.9 us
  between operations: 1.35 us -> 0.64 us
    unnamed x20 -> x4, local copies, waits for them, and re-layouts: 7.28 us -> 2.5 us
    pallas_call x1, Pallas kernels: 14.7 us -> 13.9 us  [local(): pl.pallas_call(body, out_shape=out_shape, in_specs=[hbm] * 8, out_specs=(...]
where the time goes in v2:
time: 17.2 us; the launch traced here: 17 us
  Pallas kernels  13.9 us (81%)
  local copies, waits for them, and re-layouts  2.5 us (15%)
  between operations  0.64 us (4%)
    pallas_call x1, Pallas kernels, local(): pl.pallas_call(body, out_shape=out_shape, in_specs=[hbm] * 8, out_specs=(...  13.9 us
    unnamed x4, local copies, waits for them, and re-layouts  2.5 us

profile of v2, /device:TPU:0, one launch (start us, length us, event | category | flops | bytes accessed | tf_op | source)
XLA Modules:
  0.0 17.0 jit_solution(15490530634931117999)
XLA Ops:
  0.6 13.9 %shard_map.111 = (f32[2,1,4,1024]{3,2,1,0:T(4,128)S(1)}, f32[3,1,4,1024]{3,2,1,0:T(4,128)S(1)}, f32[7,1,4,1024]{3,2,1,0:T(4,128)S(1)}, f32[3,32,128]{2,1,0:T(8,128)S(1)}) custom-call(f32[5,32,128]{2,1,0:T(8,128)} %refs_0_.1, f32[2,1,4,1024]{3,2,1,0:T(4,128)} %refs_1_.1, f32[3,1,4,1024]{3,2,1,0:T(4,128)} %refs_2_.1, f32[1,4,1024]{2,1,0:T(4,128)} %refs_3_.1, ...), custom_call_target="tpu_custom_call" | custom-call | tf_op jit(solution)/shard_map/pallas_call | solution.py:397
  14.5 0.6 %copy.16 = f32[2,1,4,1024]{3,2,1,0:T(4,128)} copy(f32[2,1,4,1024]{3,2,1,0:T(4,128)S(1)} %get-tuple-element.8) | data formatting | bytes 65536
  15.1 0.6 %copy.17 = f32[3,1,4,1024]{3,2,1,0:T(4,128)} copy(f32[3,1,4,1024]{3,2,1,0:T(4,128)S(1)} %get-tuple-element.9) | data formatting | bytes 98304
  15.8 0.6 %copy.18 = f32[7,1,4,1024]{3,2,1,0:T(4,128)} copy(f32[7,1,4,1024]{3,2,1,0:T(4,128)S(1)} %get-tuple-element.10) | data formatting | bytes 229376
  16.4 0.6 %copy.19 = f32[3,32,128]{2,1,0:T(8,128)} copy(f32[3,32,128]{2,1,0:T(8,128)S(1)} %get-tuple-element.11) | data formatting | bytes 98304

commit v3 on v2

--- a/solution.py
+++ b/solution.py
@@ -87,7 +87,7 @@
     cols,
     skin_in, motion_in, tensor_in, weight_in, strength_in, warm_in, flags_in, source_in,
     motion_out, tensor_out, warm_out, ocean_out,
-    B, TS, TSS, HF, F, K, KS, G, D, DS, send, recv,
+    B, TS, TSS, HF, F, R, RS, K, KS, G, D, DS, send, recv,
     skin, motion, tensor, weight, strength, warm, flags, source, loaded,
 ):
     pairs = (
@@ -109,7 +109,7 @@
     diagonal_north = ((me_r + 1, west[1]), (me_r + 1, east[1]))
     diagonal_south = ((me_r - 1, west[1]), (me_r - 1, east[1]))
 
-    F[:, :, 8:16, :] = jnp.zeros((9, 4, 8, 128), jnp.float32)
+    R[...] = jnp.zeros((2, 9, 8, 128), jnp.float32)
     K[:, :, 8:16, :] = jnp.zeros((2, 4, 8, 128), jnp.float32)
 
     barrier = pltpu.get_barrier_semaphore()
@@ -184,15 +184,40 @@
         F[7, q, 0:8] = AIR_DRAG * skin[3, at, :] + WATER_DRAG * skin[1, at, :]
         F[8, q, 0:8] = AIR_DRAG * skin[4, at, :] + WATER_DRAG * skin[2, at, :]
 
+    pair = lax.broadcasted_iota(jnp.int32, (8, 128), 0) // 2
+
+    def pack_rows(low, high):
+        for p in range(low, high):
+            first_rows = F[p, 0]
+            last_rows = F[p, 0]
+            for q in range(1, 4):
+                turned = pltpu.roll(F[p, q], 2 * q, 0)
+                first_rows = jnp.where(pair == q, turned, first_rows)
+                last_rows = jnp.where(pair == q - 1, turned, last_rows)
+            RS[0, p] = first_rows
+            RS[1, p] = last_rows
+
+    pack_rows(7, 9)
+    force_north = remote(12, RS.at[1, 7:9], R.at[1, 7:9], north)
+    force_south = remote(13, RS.at[0, 7:9], R.at[0, 7:9], south)
+
+    @pl.when(has_north)
+    def _():
+        force_north.start()
+
+    @pl.when(has_south)
+    def _():
+        force_south.start()
+
     slots_west.wait_recv()
     for p in range(7):
         held = [jnp.where(block_covered[b], B[block_index[b], p], 0.0) for b in range(4)]
         held = transpose4(held)
         for q in range(4):
             F[p, q, 0:8] = held[q]
-
-    rows_north = remote(4, F.at[:, :, 6:8, :], F.at[:, :, 14:16, :], north)
-    rows_south = remote(5, F.at[:, :, 0:2, :], F.at[:, :, 8:10, :], south)
+    pack_rows(0, 7)
+    rows_north = remote(4, RS.at[1, 0:7], R.at[1, 0:7], north)
+    rows_south = remote(5, RS.at[0, 0:7], R.at[0, 0:7], south)
 
     @pl.when(has_north)
     def _():
@@ -257,12 +282,12 @@
 
     @pl.when(has_south)
     def _():
-        for copy in (rows_north, *corners_north):
+        for copy in (rows_north, force_north, *corners_north):
             copy.wait_recv()
 
     @pl.when(has_north)
     def _():
-        for copy in (rows_south, *corners_south):
+        for copy in (rows_south, force_south, *corners_south):
             copy.wait_recv()
 
     wide = lax.broadcasted_iota(jnp.int32, (16, 128), 1) // 8
@@ -274,7 +299,11 @@
             side = jnp.where(wide == p, from_e, jnp.where(wide == (p + 15) % 16, from_w, 0.0))
             if p:
                 side = pltpu.roll(side, 128 - 8 * p, 1)
-            planes.append(jnp.concatenate([F[p, q], side], axis=1))
+            beyond = jnp.where(pair == q, R[0, p], jnp.where(pair == (q + 3) % 4, R[1, p], 0.0))
+            if q:
+                beyond = pltpu.roll(beyond, 8 - 2 * q, 0)
+            center = jnp.concatenate([F[p, q], beyond], axis=0)
+            planes.append(jnp.concatenate([center, side], axis=1))
         for p in range(5):
             G[p, q] = planes[p]
         mass = planes[5]
@@ -369,12 +398,12 @@
 
     @pl.when(has_north)
     def _():
-        for copy in (rows_north, *corners_north):
+        for copy in (rows_north, force_north, *corners_north):
             copy.wait_send()
 
     @pl.when(has_south)
     def _():
-        for copy in (rows_south, *corners_south):
+        for copy in (rows_south, force_south, *corners_south):
             copy.wait_send()
 
 
@@ -404,14 +433,16 @@
                 pltpu.VMEM((6, 8, 128), f32),
                 pltpu.VMEM((2, 8, 128), f32),
                 pltpu.VMEM((6, 8, 128), f32),
-                pltpu.VMEM((9, 4, 16, 128), f32),
+                pltpu.VMEM((9, 4, 8, 128), f32),
+                pltpu.VMEM((2, 9, 8, 128), f32),
+                pltpu.VMEM((2, 9, 8, 128), f32),
                 pltpu.VMEM((2, 4, 16, 128), f32),
                 pltpu.VMEM((2, 4, 8, 128), f32),
                 pltpu.VMEM((10, 4, 16, 256), f32),
                 pltpu.VMEM((6, 5, 8, 128), f32),
                 pltpu.VMEM((2, 5, 8, 128), f32),
-                pltpu.SemaphoreType.DMA((12,)),
-                pltpu.SemaphoreType.DMA((12,)),
+                pltpu.SemaphoreType.DMA((14,)),
+                pltpu.SemaphoreType.DMA((14,)),
                 *(pltpu.VMEM(a.shape, f32) for a in (skin, motion, tensor, weight, strength, warm)),
                 *(pltpu.SMEM(a.shape, jnp.int32) for a in (flags, source)),
                 pltpu.SemaphoreType.DMA((8,)),

time: 17.2 us -> 16.8 us (0.977)
  Pallas kernels: 13.9 us -> 13.5 us
    pallas_call x1, Pallas kernels: 13.9 us -> 13.5 us  [local(): pl.pallas_call(body, out_shape=out_shape, in_specs=[hbm] * 8, out_specs=(...]
where the time goes in v3:
time: 16.8 us; the launch traced here: 16.7 us
  Pallas kernels  13.5 us (80%)
  local copies, waits for them, and re-layouts  2.5 us (15%)
  between operations  0.64 us (4%)
    pallas_call x1, Pallas kernels, local(): pl.pallas_call(body, out_shape=out_shape, in_specs=[hbm] * 8, out_specs=(...  13.5 us
    unnamed x4, local copies, waits for them, and re-layouts  2.5 us

profile of v3, /device:TPU:0, one launch (start us, length us, event | category | flops | bytes accessed | tf_op | source)
XLA Modules:
  0.0 16.7 jit_solution(16846782169367655517)
XLA Ops:
  0.6 13.5 %shard_map.111 = (f32[2,1,4,1024]{3,2,1,0:T(4,128)S(1)}, f32[3,1,4,1024]{3,2,1,0:T(4,128)S(1)}, f32[7,1,4,1024]{3,2,1,0:T(4,128)S(1)}, f32[3,32,128]{2,1,0:T(8,128)S(1)}) custom-call(f32[5,32,128]{2,1,0:T(8,128)} %refs_0_.1, f32[2,1,4,1024]{3,2,1,0:T(4,128)} %refs_1_.1, f32[3,1,4,1024]{3,2,1,0:T(4,128)} %refs_2_.1, f32[1,4,1024]{2,1,0:T(4,128)} %refs_3_.1, ...), custom_call_target="tpu_custom_call" | custom-call | tf_op jit(solution)/shard_map/pallas_call | solution.py:426
  14.2 0.6 %copy.16 = f32[2,1,4,1024]{3,2,1,0:T(4,128)} copy(f32[2,1,4,1024]{3,2,1,0:T(4,128)S(1)} %get-tuple-element.8) | data formatting | bytes 65536
  14.8 0.6 %copy.17 = f32[3,1,4,1024]{3,2,1,0:T(4,128)} copy(f32[3,1,4,1024]{3,2,1,0:T(4,128)S(1)} %get-tuple-element.9) | data formatting | bytes 98304
  15.4 0.6 %copy.18 = f32[7,1,4,1024]{3,2,1,0:T(4,128)} copy(f32[7,1,4,1024]{3,2,1,0:T(4,128)S(1)} %get-tuple-element.10) | data formatting | bytes 229376
  16.1 0.6 %copy.19 = f32[3,32,128]{2,1,0:T(8,128)} copy(f32[3,32,128]{2,1,0:T(8,128)S(1)} %get-tuple-element.11) | data formatting | bytes 98304
